TPU v7x, 32 devices: a whole 2x2x4 slice. The times are simulated.
32 devices in a mesh: peer: 16 (over z, y, core), grp: 2 (over x).
Axes of the slice: x: 2, y: 2, z: 4, core: 2. Of those that a mesh axis runs over, the one named last changes fastest.
Arguments:
- images: bfloat16 [2, 16, 2, 8, 32, 384], P(None, 'peer', 'grp'), may hold values from -6 to 6
- cotangent: bfloat16 [2, 16, 2, 8, 32, 384], P(None, 'peer', 'grp'), may hold values from -6 to 6
- dw_kernel: float32 [16, 49, 384], P('peer', None, 'grp'), may hold values from -0.875 to 0.875
- chan_vec: float32 [16, 5, 384], P('peer', None, 'grp'), may hold values from 0.25 to 1.5
- w_in: float32 [16, 384, 1536], P('peer', 'grp'), may hold values from -0.3125 to 0.3125
- b_in: float32 [16, 1536], P('peer', 'grp'), may hold values from -3 to 3
- w_out: float32 [16, 1536, 384], P('peer', 'grp'), may hold values from -0.15625 to 0.15625
- mom_kernel: float32 [16, 49, 384], P('peer', None, 'grp'), may hold values from -300 to 300
- mom_chan: float32 [16, 5, 384], P('peer', None, 'grp'), may hold values from -300 to 300
- mom_in: float32 [16, 384, 1536], P('peer', 'grp'), may hold values from -300 to 300
- mom_bin: float32 [16, 1536], P('peer', 'grp'), may hold values from -300 to 300
- mom_out: float32 [16, 1536, 384], P('peer', 'grp'), may hold values from -300 to 300
Outputs:
- new_kernel: float32 [16, 49, 384], P('peer', None, 'grp')
- new_chan: float32 [16, 5, 384], P('peer', None, 'grp')
- new_in: float32 [16, 384, 1536], P('peer', 'grp')
- new_bin: float32 [16, 1536], P('peer', 'grp')
- new_out: float32 [16, 1536, 384], P('peer', 'grp')
- features: bfloat16 [16, 2, 8, 32, 384], P('peer', 'grp')
All inputs are finite; a program needn't handle non-finite values.
Results may differ from a plain program's by a relative error of at most 0.01.
Values may be sent and summed in bfloat16 or wider, within the bound.
A program may use at most 64 MiB of HBM per device.

v0:
```python
import math

import jax
import jax.numpy as jnp
from jax import lax
from jax.experimental import pallas as pl
from jax.experimental.pallas import tpu as pltpu
from jax.sharding import PartitionSpec as P

STEPS = 2


EPS = 1e-06
MOMENTUM = 0.9
RATE = 0.0005
SQRT_HALF = 0.7071067811865476
INV_ROOT_TWO_PI = 0.3989422804014327


def passed_along(block, axis, distance):
    devices = range(lax.axis_size(axis))
    route = [((i - distance) % len(devices), i) for i in devices]
    return lax.ppermute(block, axis, route)


def depthwise(field, kernel):
    channels = kernel.shape[-1]
    reach = math.isqrt(kernel.shape[0])
    margin = reach // 2
    filter_taps = kernel.reshape(reach, reach, 1, channels)
    return lax.conv_general_dilated(
        field,
        filter_taps,
        (1, 1),
        ((margin, margin), (margin, margin)),
        dimension_numbers=("NHWC", "HWIO", "NHWC"),
        feature_group_count=channels,
        precision=lax.Precision.HIGHEST,
    )


def gelu_value(value):
    return 0.5 * value * (1.0 + lax.erf(value * SQRT_HALF))


def gelu_slope(value):
    return (
        0.5 * (1.0 + lax.erf(value * SQRT_HALF))
        + value * jnp.exp(-0.5 * value * value) * INV_ROOT_TWO_PI
    )


def channel_front(image, kernel, chan):
    height, width, channels = image.shape
    field = image.astype(jnp.float32)[None]
    conv = depthwise(field, kernel)[0].reshape(height * width, channels) + chan[0]
    center = conv - jnp.mean(conv, axis=-1, keepdims=True)
    spread = lax.rsqrt(jnp.mean(center * center, axis=-1, keepdims=True) + EPS)
    scaled = center * spread
    normed = (scaled * chan[1] + chan[2]).astype(jnp.bfloat16)
    return (field, scaled, spread, normed)


def channel_back(field, scaled, spread, dnormed, chan, kernel, bias_grad, scale_grad):
    d_gain = jnp.sum(dnormed * scaled, axis=0)
    d_shift = jnp.sum(dnormed, axis=0)
    dscaled = dnormed * chan[1]
    dconv = spread * (
        dscaled
        - jnp.mean(dscaled, axis=-1, keepdims=True)
        - scaled * jnp.mean(dscaled * scaled, axis=-1, keepdims=True)
    )
    d_bias = jnp.sum(dconv, axis=0)
    _, pullback = jax.vjp(lambda taps: depthwise(field, taps), kernel)
    (d_kernel,) = pullback(dconv.reshape(field.shape))
    d_chan = jnp.stack([d_bias, d_gain, d_shift, bias_grad, scale_grad])
    return (d_kernel, d_chan)


def per_device(
    images,
    cotangent,
    dw_kernel,
    chan_vec,
    w_in,
    b_in,
    w_out,
    mom_kernel,
    mom_chan,
    mom_in,
    mom_bin,
    mom_out,
):
    params = (dw_kernel[0], chan_vec[0], w_in[0], b_in[0], w_out[0])
    moments = (mom_kernel[0], mom_chan[0], mom_in[0], mom_bin[0], mom_out[0])
    features = None
    for round_index in range(STEPS):
        kernel, chan, bias_in = (
            lax.all_gather(params[0], "grp", axis=1, tiled=True),
            lax.all_gather(params[1], "grp", axis=1, tiled=True),
            lax.all_gather(params[3], "grp", axis=0, tiled=True),
        )
        in_shard = params[2].astype(jnp.bfloat16)
        out_shard = params[4].astype(jnp.bfloat16)
        image = images[round_index, 0, 0]
        height, width, channels = image.shape
        rows = height * width
        field, scaled, spread, normed = channel_front(image, kernel, chan)
        w_in_full, w_out_full = (
            lax.all_gather(in_shard, "grp", axis=0, tiled=True),
            lax.all_gather(out_shard, "grp", axis=0, tiled=True),
        )
        pre = jnp.dot(normed, w_in_full, preferred_element_type=jnp.float32) + bias_in
        hidden = gelu_value(pre).astype(jnp.bfloat16)
        mlp = jnp.dot(hidden, w_out_full, preferred_element_type=jnp.float32) + chan[3]
        features = (image.reshape(rows, channels).astype(jnp.float32) + chan[4] * mlp).astype(
            jnp.bfloat16
        )
        cot = cotangent[round_index, 0, 0].reshape(rows, channels).astype(jnp.float32)
        bias_grad = jnp.sum(cot * chan[4], axis=0)
        scale_grad = jnp.sum(cot * mlp, axis=0)
        dmlp = (cot * chan[4]).astype(jnp.bfloat16)
        g_out = jnp.dot(hidden.T, dmlp, preferred_element_type=jnp.float32)
        dhid = jnp.dot(dmlp, w_out_full.T, preferred_element_type=jnp.float32)
        dpre = (dhid * gelu_slope(pre)).astype(jnp.bfloat16)
        g_bin = jnp.sum(dpre.astype(jnp.float32), axis=0)
        g_in = jnp.dot(normed.T, dpre, preferred_element_type=jnp.float32)
        dnormed = jnp.dot(dpre, w_in_full.T, preferred_element_type=jnp.float32)
        d_kernel, d_chan = channel_back(
            field, scaled, spread, dnormed, chan, kernel, bias_grad, scale_grad
        )
        sum_kernel, sum_chan, sum_in, sum_bin, sum_out = (
            lax.psum_scatter(
                d_kernel.astype(jnp.bfloat16), "grp", scatter_dimension=1, tiled=True
            ).astype(jnp.float32),
            lax.psum_scatter(
                d_chan.astype(jnp.bfloat16), "grp", scatter_dimension=1, tiled=True
            ).astype(jnp.float32),
            lax.psum_scatter(
                g_in.astype(jnp.bfloat16), "grp", scatter_dimension=0, tiled=True
            ).astype(jnp.float32),
            lax.psum_scatter(
                g_bin.astype(jnp.bfloat16), "grp", scatter_dimension=0, tiled=True
            ).astype(jnp.float32),
            lax.psum_scatter(
                g_out.astype(jnp.bfloat16), "grp", scatter_dimension=0, tiled=True
            ).astype(jnp.float32),
        )
        summed = (sum_kernel, sum_chan, sum_in, sum_bin, sum_out)
        moments = tuple((MOMENTUM * old + grad for old, grad in zip(moments, summed)))
        stepped = tuple((value - RATE * moment for value, moment in zip(params, moments)))
        partner = passed_along(
            (stepped[0], stepped[1], stepped[2], stepped[3], stepped[4]), "peer", 2**round_index
        )
        params = tuple((0.5 * (mine + theirs) for mine, theirs in zip(stepped, partner)))
    return (
        params[0][None],
        params[1][None],
        params[2][None],
        params[3][None],
        params[4][None],
        features.reshape(1, 1, height, width, channels),
    )


BF = jnp.bfloat16
F32 = jnp.float32
CHAN_ROW = 56
SMALL_ROWS = 64
CUT = 256
DEVICE = pl.DeviceIdType.MESH


def dot(a, b, over_a=1, over_b=0):
    return lax.dot_general(
        a, b, (((over_a,), (over_b,)), ((), ())), preferred_element_type=F32
    )


def fused_kernel(
    shape,
    image_ref, cot_ref, kernel_ref, chan_ref, win_ref, bin_ref, wout_ref,
    mkernel_ref, mchan_ref, min_ref, mbin_ref, mout_ref,
    okernel_ref, ochan_ref, oin_ref, obin_ref, oout_ref, ofeat_ref,
    small_mine, small_theirs, small_p, small_m, shifted, scaled_ref, spread_ref,
    normed, cot_theirs, dmlp, hidden, dpre, mlp_ref, mlp_out, mlp_in,
    dnorm_mine, dnorm_out, dnorm_in, dconv_ref, tap_grad, small_grad, grad_out, grad_in,
    gossip_small_out, gossip_small_in, bias_p, bias_m, bias_out, bias_in, bias_grad_ref,
    w_stage, m_stage, m_theirs, w_in_low, w_in_full, m_in_full, w_out_low, w_out_full, m_out_full,
    q_out_send, q_out_recv, q_in_send, q_in_recv, last_send, last_recv,
    send_sem, recv_sem,
):
    height, width, channels, hid = shape
    rows = height * width
    half = channels // 2
    reach = math.isqrt(kernel_ref.shape[0])
    margin = reach // 2
    taps = reach * reach
    peers = lax.axis_size("peer")
    me = lax.axis_index("peer")
    grp = lax.axis_index("grp")
    other = 1 - grp
    pair = (me, other)

    barrier = pltpu.get_barrier_semaphore()
    pl.semaphore_signal(barrier, inc=1, device_id=pair, device_id_type=DEVICE)
    for step in range(STEPS):
        source = (lax.rem(me + peers - 2**step, peers), grp)
        pl.semaphore_signal(barrier, inc=1, device_id=source, device_id_type=DEVICE)

    started = []

    def push(src, dst, device):
        at = len(started)
        copy = pltpu.make_async_remote_copy(
            src_ref=src, dst_ref=dst, send_sem=send_sem.at[at], recv_sem=recv_sem.at[at],
            device_id=device, device_id_type=DEVICE,
        )
        copy.start()
        started.append(copy)
        return copy

    my_rows = pl.ds(pl.multiple_of(grp * half, 16), half)
    their_rows = pl.ds(pl.multiple_of(other * half, 16), half)
    my_cols = pl.ds(pl.multiple_of(grp * hid, 128), hid)
    their_cols = pl.ds(pl.multiple_of(other * hid, 128), hid)

    small_mine[...] = jnp.zeros_like(small_mine)
    small_mine[0, 0:taps, :] = kernel_ref[...]
    small_mine[0, CHAN_ROW : CHAN_ROW + 5, :] = chan_ref[...]
    small_mine[1, 0:taps, :] = mkernel_ref[...]
    small_mine[1, CHAN_ROW : CHAN_ROW + 5, :] = mchan_ref[...]
    w_stage[...] = win_ref[:, their_cols].astype(BF)
    pl.semaphore_wait(barrier, 1 + STEPS)
    small_copy = push(small_mine, small_theirs, pair)
    w_copy = push(w_stage, w_in_low.at[0, my_rows, :], pair)

    w_in_low[0, my_rows, :] = win_ref[:, my_cols].astype(BF)
    w_in_full[my_rows, :] = win_ref[:, my_cols]
    m_in_full[my_rows, :] = min_ref[:, my_cols]
    m_stage[...] = min_ref[:, their_cols].astype(BF)
    w_out_low[0] = wout_ref[...].astype(BF)
    bias_p[...] = bin_ref[...]
    bias_m[...] = mbin_ref[...]

    def shift_rows(step):
        shifted[:, 0:margin] = jnp.zeros((reach, margin, width, channels), F32)
        shifted[:, margin + height :] = jnp.zeros((reach, margin, width, channels), F32)
        column = lax.broadcasted_iota(jnp.int32, (width, channels), 0)

        def body(i, _):
            x = image_ref[step, pl.ds(pl.multiple_of(i * width, width), width), :].astype(F32)
            for j in range(reach):
                off = j - margin
                moved = x if off == 0 else pltpu.roll(x, (-off) % width, 0)
                inside = (column + off >= 0) & (column + off < width)
                shifted[j, i + margin] = jnp.where(inside, moved, 0.0)
            return 0

        lax.fori_loop(0, height, body, 0)

    def front(step):
        bias, gain, shift = (small_p[CHAN_ROW + k : CHAN_ROW + k + 1, :] for k in range(3))

        def body(i, _):
            conv = jnp.zeros((width, channels), F32)
            for t in range(taps):
                conv = conv + shifted[t % reach, i + t // reach] * small_p[t : t + 1, :]
            conv = conv + bias
            center = conv - jnp.mean(conv, axis=-1, keepdims=True)
            spread = lax.rsqrt(jnp.mean(center * center, axis=-1, keepdims=True) + EPS)
            scaled = center * spread
            at = pl.ds(pl.multiple_of(i * width, width), width)
            scaled_ref[at, :] = scaled
            spread_ref[at, :] = spread
            normed[step, at, :] = (scaled * gain + shift).astype(BF)
            return 0

        lax.fori_loop(0, height, body, 0)

    def through(step, place):
        at = slice(place * rows, (place + 1) * rows)
        scale = small_p[CHAN_ROW + 4 : CHAN_ROW + 5, :]
        cot = (cot_ref[step] if place == 0 else cot_theirs[step]).astype(F32)
        dmlp[at, :] = (cot * scale).astype(BF)

        def body(c, _):
            cut = pl.ds(pl.multiple_of(c * CUT, CUT), CUT)
            pre = dot(normed[step, at, :], w_in_low[step, :, cut]) + bias_p[0:1, cut]
            bell = 0.5 * (1.0 + lax.erf(pre * SQRT_HALF))
            hidden[at, cut] = (pre * bell).astype(BF)
            slope = bell + pre * jnp.exp(-0.5 * pre * pre) * INV_ROOT_TWO_PI
            dhid = dot(dmlp[at, :], w_out_low[step, cut, :], 1, 1)
            dpre[at, cut] = (dhid * slope).astype(BF)
            return 0

        lax.fori_loop(0, hid // CUT, body, 0)
        dnorm = dot(dpre[at, :], w_in_low[step], 1, 1)
        return cot, dnorm, at

    def take_gossip(step, low):
        for copy in gossip["out"]:
            copy.wait_recv()
        value = 0.5 * (w_out_full[...] + q_out_recv[step].astype(F32))
        w_out_full[...] = value
        low[...] = value.astype(low.dtype)

    shift_rows(0)
    small_copy.wait_recv()
    for k, full in enumerate((small_p, small_m)):
        mine, theirs = small_mine[k], small_theirs[k]
        first = jnp.where(grp == 0, mine, theirs)
        second = jnp.where(grp == 0, theirs, mine)
        full[...] = jnp.concatenate([first, second], axis=1)

    for step in range(STEPS):
        front(step)
        normed_copy = push(normed.at[step, 0:rows], normed.at[step, rows : 2 * rows], pair)
        if step == 0:
            cot_copy = push(cot_ref.at[0], cot_theirs.at[0], pair)
            w_copy.wait_recv()
        else:
            take_gossip(0, w_out_low.at[1])
            for copy in gossip["in"]:
                copy.wait_recv()
            value = 0.5 * (w_in_full[...] + q_in_recv[0].astype(F32))
            w_in_full[...] = value
            w_in_low[1] = value.astype(BF)
            gossip["bias"].wait_recv()
            bias_p[...] = 0.5 * (bias_p[...] + bias_in[0, 0:1, :])

        cot, dnorm, at = through(step, 0)
        dnorm_mine[...] = dnorm
        mlp = dot(hidden[at, :], w_out_low[step])
        mlp_ref[...] = mlp
        scale_grad = jnp.sum(cot * mlp, axis=0, keepdims=True)
        cot_sum = jnp.sum(cot, axis=0, keepdims=True)
        scale_grad = scale_grad + cot_sum * small_p[CHAN_ROW + 3 : CHAN_ROW + 4, :]
        bias_grad = jnp.sum(cot * small_p[CHAN_ROW + 4 : CHAN_ROW + 5, :], axis=0, keepdims=True)

        normed_copy.wait_recv()
        cot_copy.wait_recv()
        cot, dnorm, at = through(step, 1)
        dnorm_out[step] = dnorm.astype(BF)
        dnorm_copy = push(dnorm_out.at[step], dnorm_in.at[step], pair)
        mlp = dot(hidden[at, :], w_out_low[step])
        scale_grad = scale_grad + jnp.sum(cot * mlp, axis=0, keepdims=True)
        if step == STEPS - 1:
            mlp_out[...] = mlp.astype(BF)
            mlp_copy = push(mlp_out, mlp_in, pair)
        else:
            m_copy = push(m_stage, m_theirs, pair)

        onward = (lax.rem(me + 2**step, peers), grp)
        gossip = {"out": [], "in": []}
        if step == 0:
            m_out_full[...] = mout_ref[...]
            w_out_full[...] = wout_ref[...]
        for c in range(hid // CUT):
            cut = slice(c * CUT, (c + 1) * CUT)
            grad = dot(hidden[:, cut], dmlp[...], 0, 0)
            moment = MOMENTUM * m_out_full[cut, :] + grad
            m_out_full[cut, :] = moment
            stepped = w_out_full[cut, :] - RATE * moment
            w_out_full[cut, :] = stepped
            q_out_send[step, cut, :] = stepped.astype(BF)
            gossip["out"].append(push(q_out_send.at[step, cut], q_out_recv.at[step, cut], onward))
        bias_moment = MOMENTUM * bias_m[...] + jnp.sum(dpre[...].astype(F32), axis=0, keepdims=True)
        bias_m[...] = bias_moment
        bias_p[...] = bias_p[...] - RATE * bias_moment
        bias_out[step] = jnp.broadcast_to(bias_p[...], bias_out.shape[1:])
        gossip["bias"] = push(bias_out.at[step], bias_in.at[step], onward)

        if step == 0:
            m_copy.wait_recv()
            m_in_full[their_rows, :] = m_theirs[...].astype(F32)
            w_in_full[their_rows, :] = w_in_low[0, their_rows, :].astype(F32)
        pieces = channels // 128
        for c in range(pieces):
            cut = slice(c * 128, (c + 1) * 128)
            grad = dot(normed[step, :, cut], dpre[...], 0, 0)
            moment = MOMENTUM * m_in_full[cut, :] + grad
            m_in_full[cut, :] = moment
            stepped = w_in_full[cut, :] - RATE * moment
            w_in_full[cut, :] = stepped
            q_in_send[step, cut, :] = stepped.astype(BF)
            gossip["in"].append(push(q_in_send.at[step, cut], q_in_recv.at[step, cut], onward))

        dnorm_copy.wait_recv()
        gain = small_p[CHAN_ROW + 1 : CHAN_ROW + 2, :]
        zero = jnp.zeros((1, channels), F32)

        def back(i, sums):
            at = pl.ds(pl.multiple_of(i * width, width), width)
            dn = dnorm_mine[at, :] + dnorm_in[step, at, :].astype(F32)
            scaled = scaled_ref[at, :]
            ds = dn * gain
            dconv = spread_ref[at, :] * (
                ds
                - jnp.mean(ds, axis=-1, keepdims=True)
                - scaled * jnp.mean(ds * scaled, axis=-1, keepdims=True)
            )
            dconv_ref[i] = dconv
            return (
                sums[0] + jnp.sum(dconv, axis=0, keepdims=True),
                sums[1] + jnp.sum(dn * scaled, axis=0, keepdims=True),
                sums[2] + jnp.sum(dn, axis=0, keepdims=True),
            )

        sums = lax.fori_loop(0, height, back, (zero, zero, zero))

        def tap_column(j, _):
            for b in range(channels // 128):
                lanes = slice(b * 128, (b + 1) * 128)
                got = []
                for d in range(reach):
                    total = jnp.zeros((width, 128), F32)
                    for i in range(height):
                        total = total + shifted[j, i + d, :, lanes] * dconv_ref[i, :, lanes]
                    got.append(jnp.sum(total, axis=0, keepdims=True))
                for d in range(reach):
                    tap_grad[j, d : d + 1, lanes] = got[d]
            return 0

        lax.fori_loop(0, reach, tap_column, 0)
        small_grad[...] = jnp.zeros_like(small_grad)
        for t in range(taps):
            small_grad[t : t + 1, :] = tap_grad[t % reach, t // reach : t // reach + 1, :]
        for k, value in enumerate((*sums, bias_grad, scale_grad)):
            small_grad[CHAN_ROW + k : CHAN_ROW + k + 1, :] = value
        grad_out[step] = small_grad[...].astype(BF)
        grad_copy = push(grad_out.at[step], grad_in.at[step], pair)
        if step + 1 < STEPS:
            shift_rows(step + 1)
        else:
            mlp_copy.wait_recv()
            mlp = mlp_ref[...] + mlp_in[...].astype(F32) + small_p[CHAN_ROW + 3 : CHAN_ROW + 4, :]
            ofeat_ref[...] = (
                image_ref[step].astype(F32) + small_p[CHAN_ROW + 4 : CHAN_ROW + 5, :] * mlp
            ).astype(BF)
        grad_copy.wait_recv()
        moment = MOMENTUM * small_m[...] + (grad_out[step].astype(F32) + grad_in[step].astype(F32))
        small_m[...] = moment
        stepped = small_p[...] - RATE * moment
        gossip_small_out[step] = stepped.astype(BF)
        small_gossip = push(gossip_small_out.at[step], gossip_small_in.at[step], onward)
        if step + 1 < STEPS:
            cot_copy = push(cot_ref.at[step + 1], cot_theirs.at[step + 1], pair)
        small_gossip.wait_recv()
        small_p[...] = 0.5 * (stepped + gossip_small_in[step].astype(F32))

    def mine_of(value):
        return jnp.where(grp == 0, value[:, 0:half], value[:, half:])

    okernel_ref[...] = mine_of(small_p[0:taps, :])
    ochan_ref[...] = mine_of(small_p[CHAN_ROW : CHAN_ROW + 5, :])
    last = STEPS - 1
    take_gossip(last, oout_ref)
    gossip["bias"].wait_recv()
    obin_ref[...] = 0.5 * (bias_p[...] + bias_in[last, 0:1, :])
    for copy in gossip["in"]:
        copy.wait_recv()
    last_send[...] = (
        0.5 * (w_in_full[their_rows, :] + q_in_recv[last, their_rows, :].astype(F32))
    ).astype(BF)
    last_copy = push(last_send, last_recv, pair)
    oin_ref[:, my_cols] = 0.5 * (w_in_full[my_rows, :] + q_in_recv[last, my_rows, :].astype(F32))
    last_copy.wait_recv()
    oin_ref[:, their_cols] = last_recv[...].astype(F32)
    for copy in started:
        copy.wait_send()


def fused_device(
    images, cotangent, dw_kernel, chan_vec, w_in, b_in, w_out,
    mom_kernel, mom_chan, mom_in, mom_bin, mom_out,
):
    steps, _, _, height, width, channels = images.shape
    rows = height * width
    taps, half = dw_kernel.shape[1:]
    reach = math.isqrt(taps)
    margin = reach // 2
    hid = b_in.shape[1]
    V = pltpu.VMEM
    scratch = [
        V((2, SMALL_ROWS, half), F32), V((2, SMALL_ROWS, half), F32),
        V((SMALL_ROWS, channels), F32), V((SMALL_ROWS, channels), F32),
        V((reach, height + 2 * margin, width, channels), F32),
        V((rows, channels), F32), V((rows, 1), F32),
        V((steps, 2 * rows, channels), BF), V((steps, rows, channels), BF),
        V((2 * rows, channels), BF), V((2 * rows, hid), BF), V((2 * rows, hid), BF),
        V((rows, channels), F32), V((rows, channels), BF), V((rows, channels), BF),
        V((rows, channels), F32), V((steps, rows, channels), BF), V((steps, rows, channels), BF),
        V((height, width, channels), F32), V((reach, 8, channels), F32),
        V((SMALL_ROWS, channels), F32),
        V((steps, SMALL_ROWS, channels), BF), V((steps, SMALL_ROWS, channels), BF),
        V((steps, SMALL_ROWS, channels), BF), V((steps, SMALL_ROWS, channels), BF),
        V((1, hid), F32), V((1, hid), F32),
        V((steps, 8, hid), F32), V((steps, 8, hid), F32), V((1, hid), F32),
        V((half, hid), BF), V((half, hid), BF), V((half, hid), BF),
        V((steps, channels, hid), BF), V((channels, hid), F32), V((channels, hid), F32),
        V((steps, hid, channels), BF), V((hid, channels), F32), V((hid, channels), F32),
        V((steps, hid, channels), BF), V((steps, hid, channels), BF),
        V((steps, channels, hid), BF), V((steps, channels, hid), BF),
        V((half, hid), BF), V((half, hid), BF),
        pltpu.SemaphoreType.DMA((40,)), pltpu.SemaphoreType.DMA((40,)),
    ]
    shapes = [
        jax.ShapeDtypeStruct((taps, half), F32),
        jax.ShapeDtypeStruct(chan_vec.shape[1:], F32),
        jax.ShapeDtypeStruct(w_in.shape[1:], F32),
        jax.ShapeDtypeStruct((1, hid), F32),
        jax.ShapeDtypeStruct(w_out.shape[1:], F32),
        jax.ShapeDtypeStruct((rows, channels), BF),
    ]
    whole = pl.BlockSpec(memory_space=pltpu.VMEM)
    out = pl.pallas_call(
        lambda *refs: fused_kernel((height, width, channels, hid), *refs),
        out_shape=shapes,
        in_specs=[whole] * 12,
        out_specs=[whole] * 6,
        scratch_shapes=scratch,
        compiler_params=pltpu.CompilerParams(
            collective_id=0, has_side_effects=True, vmem_limit_bytes=56 * 2**20
        ),
    )(
        images.reshape(steps, rows, channels), cotangent.reshape(steps, rows, channels),
        dw_kernel[0], chan_vec[0], w_in[0], b_in, w_out[0],
        mom_kernel[0], mom_chan[0], mom_in[0], mom_bin, mom_out[0],
    )
    return (
        out[0][None], out[1][None], out[2][None], out[3], out[4][None],
        out[5].reshape(1, 1, height, width, channels),
    )


def solution(mesh):
    fused = mesh.shape["grp"] == 2 and mesh.shape["peer"] > 4
    return jax.shard_map(
        fused_device if fused else per_device,
        mesh=mesh,
        in_specs=(
            P(None, "peer", "grp", None, None, None),
            P(None, "peer", "grp", None, None, None),
            P("peer", None, "grp"),
            P("peer", None, "grp"),
            P("peer", "grp", None),
            P("peer", "grp"),
            P("peer", "grp", None),
            P("peer", None, "grp"),
            P("peer", None, "grp"),
            P("peer", "grp", None),
            P("peer", "grp"),
            P("peer", "grp", None),
        ),
        out_specs=(
            P("peer", None, "grp"),
            P("peer", None, "grp"),
            P("peer", "grp", None),
            P("peer", "grp"),
            P("peer", "grp", None),
            P("peer", "grp", None, None, None),
        ),
        check_vma=False,
    )
```

profile of v0, /device:TPU:0, one launch (start us, length us, event | category | flops | bytes accessed | tf_op | source)
XLA Modules:
  0.0 107.7 jit_solution(13720912611908948665)
XLA Ops:
  0.6 1.3 %copy_bitcast_fusion.2 = (f32[5,192]{1,0:T(8,128)}, f32[5,192]{1,0:T(8,128)}) fusion(f32[1,5,192]{2,0,1:T(1,128)} %param.20, f32[1,5,192]{2,0,1:T(1,128)} %param.15), kind=kLoop, calls=%fused_computation.2 | loop fusion | bytes 15360
  1.9 1.5 %copy_bitcast_fusion = (f32[49,192]{1,0:T(8,128)}, f32[49,192]{1,0:T(8,128)}) fusion(f32[1,49,192]{2,0,1:T(1,128)} %param.19, f32[1,49,192]{2,0,1:T(1,128)} %param.14), kind=kLoop, calls=%fused_computation | loop fusion | bytes 150528
  3.4 96.6 %shard_map.163 = (f32[49,192]{1,0:T(8,128)}, f32[5,192]{1,0:T(8,128)}, f32[192,1536]{1,0:T(8,128)}, f32[1,768]{1,0:T(1,128)}, f32[768,384]{1,0:T(8,128)}, /*index=5*/bf16[256,384]{1,0:T(8,128)(2,1)}) custom-call(bf16[2,256,384]{2,1,0:T(8,128)(2,1)} %bitcast.25, bf16[2,256,384]{2,1,0:T(8,128)(2,1)} %bitcast.26, f32[49,192]{1,0:T(8,128)} %get-tuple-element.25.refs_2_, ...), custom_call_target="tpu_custom_call" | custom-call | tf_op jit(solution)/shard_map/pallas_call | solution.py:517
  100.0 1.5 %copy.18 = f32[1,49,192]{2,0,1:T(1,128)} copy(f32[1,49,192]{2,1,0:T(8,128)} %bitcast.28) | data formatting | bytes 75264
  101.5 1.3 %copy.19 = f32[1,5,192]{2,0,1:T(1,128)} copy(f32[1,5,192]{2,1,0:T(8,128)} %bitcast.29) | data formatting | bytes 7680
  102.8 0.0 copy-start.2
  102.8 0.0 copy-start
  102.8 2.5 %copy.32 = f32[1,192,1536]{2,1,0:T(8,128)} copy(f32[1,192,1536]{2,1,0:T(8,128)} %bitcast.20) | data formatting | bytes 2359296
  105.3 0.0 copy-done.2
  105.3 0.6 copy.33
  105.9 0.0 copy-done
  105.9 0.0 copy-start.1
  105.9 1.0 copy.34
  106.9 0.1 copy-done.1
  107.0 0.7 copy.35
Async XLA Ops:
  102.8 2.5 %copy-start.2 = (f32[1,768]{1,0:T(1,128)S(1)}, f32[1,768]{1,0:T(1,128)}, u32[]{:S(2)}) copy-start(f32[1,768]{1,0:T(1,128)} %get-tuple-element.37) | copy-start | bytes 9220
  102.8 3.0 %copy-start = (f32[768,384]{1,0:T(8,128)S(1)}, f32[768,384]{1,0:T(8,128)}, u32[]{:S(2)}) copy-start(f32[768,384]{1,0:T(8,128)} %get-tuple-element.16) | copy-start | bytes 3538948
  105.9 1.1 %copy-start.1 = (bf16[256,384]{1,0:T(8,128)(2,1)S(1)}, bf16[256,384]{1,0:T(8,128)(2,1)}, u32[]{:S(2)}) copy-start(bf16[256,384]{1,0:T(8,128)(2,1)} %get-tuple-element.17) | copy-start | bytes 589828
where the time goes:
time: 108 us
  Pallas kernels  96.6 us (89%)
  local copies, waits for them, and re-layouts  10.4 us (10%)
    pallas_call x1, Pallas kernels, fused_device(): pl.pallas_call(lambda *refs: fused_kernel((height, width, channels, hid),...  96.6 us
    unnamed x14, local copies, waits for them, and re-layouts  10.4 us

commit v1 on v0

--- a/solution.py
+++ b/solution.py
@@ -188,7 +188,7 @@
     gossip_small_out, gossip_small_in, bias_p, bias_m, bias_out, bias_in, bias_grad_ref,
     w_stage, m_stage, m_theirs, w_in_low, w_in_full, m_in_full, w_out_low, w_out_full, m_out_full,
     q_out_send, q_out_recv, q_in_send, q_in_recv, last_send, last_recv,
-    send_sem, recv_sem,
+    normed_t, in_grad, m_in_rows, send_sem, recv_sem, load_sem,
 ):
     height, width, channels, hid = shape
     rows = height * width
@@ -208,6 +208,14 @@
         source = (lax.rem(me + peers - 2**step, peers), grp)
         pl.semaphore_signal(barrier, inc=1, device_id=source, device_id_type=DEVICE)
 
+    loads = [
+        pltpu.make_async_copy(src, dst, load_sem.at[k])
+        for k, (src, dst) in enumerate(
+            ((wout_ref, w_out_full), (mout_ref, m_out_full), (min_ref, m_in_rows))
+        )
+    ]
+    for load in loads:
+        load.start()
     started = []
 
     def push(src, dst, device):
@@ -226,20 +234,17 @@
     their_cols = pl.ds(pl.multiple_of(other * hid, 128), hid)
 
     small_mine[...] = jnp.zeros_like(small_mine)
-    small_mine[0, 0:taps, :] = kernel_ref[...]
-    small_mine[0, CHAN_ROW : CHAN_ROW + 5, :] = chan_ref[...]
-    small_mine[1, 0:taps, :] = mkernel_ref[...]
-    small_mine[1, CHAN_ROW : CHAN_ROW + 5, :] = mchan_ref[...]
+    small_mine[0, 0:taps, :] = kernel_ref[:, 0, :]
+    small_mine[0, CHAN_ROW : CHAN_ROW + 5, :] = chan_ref[:, 0, :]
     w_stage[...] = win_ref[:, their_cols].astype(BF)
     pl.semaphore_wait(barrier, 1 + STEPS)
-    small_copy = push(small_mine, small_theirs, pair)
+    small_copy = push(small_mine.at[0], small_theirs.at[0], pair)
     w_copy = push(w_stage, w_in_low.at[0, my_rows, :], pair)
+    small_mine[1, 0:taps, :] = mkernel_ref[:, 0, :]
+    small_mine[1, CHAN_ROW : CHAN_ROW + 5, :] = mchan_ref[:, 0, :]
 
     w_in_low[0, my_rows, :] = win_ref[:, my_cols].astype(BF)
     w_in_full[my_rows, :] = win_ref[:, my_cols]
-    m_in_full[my_rows, :] = min_ref[:, my_cols]
-    m_stage[...] = min_ref[:, their_cols].astype(BF)
-    w_out_low[0] = wout_ref[...].astype(BF)
     bias_p[...] = bin_ref[...]
     bias_m[...] = mbin_ref[...]
 
@@ -276,9 +281,15 @@
             normed[step, at, :] = (scaled * gain + shift).astype(BF)
             return 0
 
-        lax.fori_loop(0, height, body, 0)
-
-    def through(step, place):
+        copies = []
+        for h in range(2):
+            lax.fori_loop(h * height // 2, (h + 1) * height // 2, body, 0)
+            at = slice(h * rows // 2, (h + 1) * rows // 2)
+            theirs = slice(rows + at.start, rows + at.stop)
+            copies.append(push(normed.at[step, at], normed.at[step, theirs], pair))
+        return copies
+
+    def through(step, place, after=None):
         at = slice(place * rows, (place + 1) * rows)
         scale = small_p[CHAN_ROW + 4 : CHAN_ROW + 5, :]
         cot = (cot_ref[step] if place == 0 else cot_theirs[step]).astype(F32)
@@ -294,68 +305,27 @@
             dpre[at, cut] = (dhid * slope).astype(BF)
             return 0
 
-        lax.fori_loop(0, hid // CUT, body, 0)
-        dnorm = dot(dpre[at, :], w_in_low[step], 1, 1)
-        return cot, dnorm, at
-
-    def take_gossip(step, low):
-        for copy in gossip["out"]:
-            copy.wait_recv()
-        value = 0.5 * (w_out_full[...] + q_out_recv[step].astype(F32))
-        w_out_full[...] = value
-        low[...] = value.astype(low.dtype)
-
-    shift_rows(0)
-    small_copy.wait_recv()
-    for k, full in enumerate((small_p, small_m)):
-        mine, theirs = small_mine[k], small_theirs[k]
-        first = jnp.where(grp == 0, mine, theirs)
-        second = jnp.where(grp == 0, theirs, mine)
-        full[...] = jnp.concatenate([first, second], axis=1)
-
-    for step in range(STEPS):
-        front(step)
-        normed_copy = push(normed.at[step, 0:rows], normed.at[step, rows : 2 * rows], pair)
-        if step == 0:
-            cot_copy = push(cot_ref.at[0], cot_theirs.at[0], pair)
-            w_copy.wait_recv()
+        if after is None:
+            lax.fori_loop(0, hid // CUT, body, 0)
         else:
-            take_gossip(0, w_out_low.at[1])
-            for copy in gossip["in"]:
-                copy.wait_recv()
-            value = 0.5 * (w_in_full[...] + q_in_recv[0].astype(F32))
-            w_in_full[...] = value
-            w_in_low[1] = value.astype(BF)
-            gossip["bias"].wait_recv()
-            bias_p[...] = 0.5 * (bias_p[...] + bias_in[0, 0:1, :])
-
-        cot, dnorm, at = through(step, 0)
-        dnorm_mine[...] = dnorm
-        mlp = dot(hidden[at, :], w_out_low[step])
-        mlp_ref[...] = mlp
-        scale_grad = jnp.sum(cot * mlp, axis=0, keepdims=True)
-        cot_sum = jnp.sum(cot, axis=0, keepdims=True)
-        scale_grad = scale_grad + cot_sum * small_p[CHAN_ROW + 3 : CHAN_ROW + 4, :]
-        bias_grad = jnp.sum(cot * small_p[CHAN_ROW + 4 : CHAN_ROW + 5, :], axis=0, keepdims=True)
-
-        normed_copy.wait_recv()
-        cot_copy.wait_recv()
-        cot, dnorm, at = through(step, 1)
-        dnorm_out[step] = dnorm.astype(BF)
-        dnorm_copy = push(dnorm_out.at[step], dnorm_in.at[step], pair)
-        mlp = dot(hidden[at, :], w_out_low[step])
-        scale_grad = scale_grad + jnp.sum(cot * mlp, axis=0, keepdims=True)
-        if step == STEPS - 1:
-            mlp_out[...] = mlp.astype(BF)
-            mlp_copy = push(mlp_out, mlp_in, pair)
-        else:
-            m_copy = push(m_stage, m_theirs, pair)
-
-        onward = (lax.rem(me + 2**step, peers), grp)
-        gossip = {"out": [], "in": []}
-        if step == 0:
-            m_out_full[...] = mout_ref[...]
-            w_out_full[...] = wout_ref[...]
+            for c in range(hid // CUT):
+                body(c, 0)
+                after(c)
+        return cot, at
+
+    def in_update(step, c, grad):
+        cut = slice(c * CUT, (c + 1) * CUT)
+        moment = MOMENTUM * m_in_full[:, cut] + grad
+        m_in_full[:, cut] = moment
+        stepped = w_in_full[:, cut] - RATE * moment
+        w_in_full[:, cut] = stepped
+        q_in_send[step, c] = stepped.astype(BF)
+        gossip["in"].append(push(q_in_send.at[step, c], q_in_recv.at[step, c], onward))
+
+    def in_gradient(step, c):
+        return dot(normed_t[...], dpre[:, c * CUT : (c + 1) * CUT])
+
+    def out_updates(step):
         for c in range(hid // CUT):
             cut = slice(c * CUT, (c + 1) * CUT)
             grad = dot(hidden[:, cut], dmlp[...], 0, 0)
@@ -365,28 +335,90 @@
             w_out_full[cut, :] = stepped
             q_out_send[step, cut, :] = stepped.astype(BF)
             gossip["out"].append(push(q_out_send.at[step, cut], q_out_recv.at[step, cut], onward))
+
+    def bias_update(step):
         bias_moment = MOMENTUM * bias_m[...] + jnp.sum(dpre[...].astype(F32), axis=0, keepdims=True)
         bias_m[...] = bias_moment
         bias_p[...] = bias_p[...] - RATE * bias_moment
         bias_out[step] = jnp.broadcast_to(bias_p[...], bias_out.shape[1:])
         gossip["bias"] = push(bias_out.at[step], bias_in.at[step], onward)
 
+    shift_rows(0)
+
+    def join(k, full):
+        mine, theirs = small_mine[k], small_theirs[k]
+        first = jnp.where(grp == 0, mine, theirs)
+        second = jnp.where(grp == 0, theirs, mine)
+        full[...] = jnp.concatenate([first, second], axis=1)
+
+    small_copy.wait_recv()
+    join(0, small_p)
+
+    for step in range(STEPS):
+        normed_copies = front(step)
         if step == 0:
-            m_copy.wait_recv()
-            m_in_full[their_rows, :] = m_theirs[...].astype(F32)
-            w_in_full[their_rows, :] = w_in_low[0, their_rows, :].astype(F32)
-        pieces = channels // 128
-        for c in range(pieces):
-            cut = slice(c * 128, (c + 1) * 128)
-            grad = dot(normed[step, :, cut], dpre[...], 0, 0)
-            moment = MOMENTUM * m_in_full[cut, :] + grad
-            m_in_full[cut, :] = moment
-            stepped = w_in_full[cut, :] - RATE * moment
-            w_in_full[cut, :] = stepped
-            q_in_send[step, cut, :] = stepped.astype(BF)
-            gossip["in"].append(push(q_in_send.at[step, cut], q_in_recv.at[step, cut], onward))
+            cot_copy = push(cot_ref.at[0], cot_theirs.at[0], pair)
+            loads[0].wait()
+            w_out_low[0] = w_out_full[...].astype(BF)
+            w_copy.wait_recv()
+        else:
+            for c, copy in enumerate(gossip["out"]):
+                cut = slice(c * CUT, (c + 1) * CUT)
+                copy.wait_recv()
+                value = 0.5 * (w_out_full[cut, :] + q_out_recv[0, cut, :].astype(F32))
+                w_out_full[cut, :] = value
+                w_out_low[1, cut, :] = value.astype(BF)
+            for c, copy in enumerate(gossip["in"]):
+                cut = slice(c * CUT, (c + 1) * CUT)
+                copy.wait_recv()
+                value = 0.5 * (w_in_full[:, cut] + q_in_recv[0, c].astype(F32))
+                w_in_full[:, cut] = value
+                w_in_low[1, :, cut] = value.astype(BF)
+            gossip["bias"].wait_recv()
+            bias_p[...] = 0.5 * (bias_p[...] + bias_in[0, 0:1, :])
+        onward = (lax.rem(me + 2**step, peers), grp)
+        gossip = {"out": [], "in": []}
+
+        cot, at = through(step, 0)
+        dnorm_mine[...] = dot(dpre[at, :], w_in_low[step], 1, 1)
+        mlp = dot(hidden[at, :], w_out_low[step])
+        mlp_ref[...] = mlp
+        normed_t[:, at] = normed[step, at, :].T
+        scale_grad = jnp.sum(cot * mlp, axis=0, keepdims=True)
+        cot_sum = jnp.sum(cot, axis=0, keepdims=True)
+        scale_grad = scale_grad + cot_sum * small_p[CHAN_ROW + 3 : CHAN_ROW + 4, :]
+        bias_grad = jnp.sum(cot * small_p[CHAN_ROW + 4 : CHAN_ROW + 5, :], axis=0, keepdims=True)
+        if step == 0:
+            loads[1].wait()
+            loads[2].wait()
+            m_in_full[my_rows, :] = m_in_rows[:, my_cols]
+            m_stage[...] = m_in_rows[:, their_cols].astype(BF)
+
+        for copy in normed_copies:
+            copy.wait_recv()
+        normed_t[:, rows : 2 * rows] = normed[step, rows : 2 * rows, :].T
+        cot_copy.wait_recv()
+        final = step == STEPS - 1
+        after = (lambda c: in_update(step, c, in_gradient(step, c))) if final else None
+        cot, at = through(step, 1, after)
+        dnorm_out[step] = dot(dpre[at, :], w_in_low[step], 1, 1).astype(BF)
+        dnorm_copy = push(dnorm_out.at[step], dnorm_in.at[step], pair)
+        out_updates(step)
+        mlp = dot(hidden[at, :], w_out_low[step])
+        scale_grad = scale_grad + jnp.sum(cot * mlp, axis=0, keepdims=True)
+        bias_update(step)
+        if final:
+            mlp_out[...] = mlp.astype(BF)
+        else:
+            for c in range(hid // CUT):
+                in_grad[:, c * CUT : (c + 1) * CUT] = in_gradient(step, c)
 
         dnorm_copy.wait_recv()
+        if final:
+            mlp_copy = push(mlp_out, mlp_in, pair)
+        else:
+            small_m_copy = push(small_mine.at[1], small_theirs.at[1], pair)
+            m_copy = push(m_stage, m_theirs, pair)
         gain = small_p[CHAN_ROW + 1 : CHAN_ROW + 2, :]
         zero = jnp.zeros((1, channels), F32)
 
@@ -432,6 +464,8 @@
         grad_copy = push(grad_out.at[step], grad_in.at[step], pair)
         if step + 1 < STEPS:
             shift_rows(step + 1)
+            small_m_copy.wait_recv()
+            join(1, small_m)
         else:
             mlp_copy.wait_recv()
             mlp = mlp_ref[...] + mlp_in[...].astype(F32) + small_p[CHAN_ROW + 3 : CHAN_ROW + 4, :]
@@ -445,30 +479,60 @@
         gossip_small_out[step] = stepped.astype(BF)
         small_gossip = push(gossip_small_out.at[step], gossip_small_in.at[step], onward)
         if step + 1 < STEPS:
+            m_copy.wait_recv()
+            m_in_full[their_rows, :] = m_theirs[...].astype(F32)
+            w_in_full[their_rows, :] = w_in_low[0, their_rows, :].astype(F32)
+            for c in range(hid // CUT):
+                in_update(step, c, in_grad[:, c * CUT : (c + 1) * CUT])
             cot_copy = push(cot_ref.at[step + 1], cot_theirs.at[step + 1], pair)
-        small_gossip.wait_recv()
-        small_p[...] = 0.5 * (stepped + gossip_small_in[step].astype(F32))
+        if not final:
+            small_gossip.wait_recv()
+            small_p[...] = 0.5 * (stepped + gossip_small_in[step].astype(F32))
+
+    last = STEPS - 1
+    last_copies = []
+    for c, copy in enumerate(gossip["in"]):
+        cut = slice(c * CUT, (c + 1) * CUT)
+        cols = pl.ds(pl.multiple_of(grp * hid + c * CUT, CUT), CUT)
+        copy.wait_recv()
+        last_send[c] = (
+            0.5 * (w_in_full[their_rows, cut] + q_in_recv[last, c, their_rows, :].astype(F32))
+        ).astype(BF)
+        last_copies.append(push(last_send.at[c], last_recv.at[c], pair))
+        oin_ref[:, cols] = 0.5 * (w_in_full[my_rows, cut] + q_in_recv[last, c, my_rows, :].astype(F32))
+    gossip["bias"].wait_recv()
+    obin_ref[...] = 0.5 * (bias_p[...] + bias_in[last, 0:1, :])
+    for c, copy in enumerate(last_copies):
+        cols = pl.ds(pl.multiple_of(other * hid + c * CUT, CUT), CUT)
+        copy.wait_recv()
+        oin_ref[:, cols] = last_recv[c].astype(F32)
+    for c, copy in enumerate(gossip["out"]):
+        cut = slice(c * CUT, (c + 1) * CUT)
+        copy.wait_recv()
+        oout_ref[cut, :] = 0.5 * (w_out_full[cut, :] + q_out_recv[last, cut, :].astype(F32))
+    small_gossip.wait_recv()
+    small_p[...] = 0.5 * (stepped + gossip_small_in[last].astype(F32))
 
     def mine_of(value):
         return jnp.where(grp == 0, value[:, 0:half], value[:, half:])
 
-    okernel_ref[...] = mine_of(small_p[0:taps, :])
-    ochan_ref[...] = mine_of(small_p[CHAN_ROW : CHAN_ROW + 5, :])
-    last = STEPS - 1
-    take_gossip(last, oout_ref)
-    gossip["bias"].wait_recv()
-    obin_ref[...] = 0.5 * (bias_p[...] + bias_in[last, 0:1, :])
-    for copy in gossip["in"]:
-        copy.wait_recv()
-    last_send[...] = (
-        0.5 * (w_in_full[their_rows, :] + q_in_recv[last, their_rows, :].astype(F32))
-    ).astype(BF)
-    last_copy = push(last_send, last_recv, pair)
-    oin_ref[:, my_cols] = 0.5 * (w_in_full[my_rows, :] + q_in_recv[last, my_rows, :].astype(F32))
-    last_copy.wait_recv()
-    oin_ref[:, their_cols] = last_recv[...].astype(F32)
+    okernel_ref[:, 0, :] = mine_of(small_p[0:taps, :])
+    ochan_ref[:, 0, :] = mine_of(small_p[CHAN_ROW : CHAN_ROW + 5, :])
     for copy in started:
         copy.wait_send()
+
+
+def write_results(*refs):
+    sems = refs[-1]
+    half = (len(refs) - 1) // 2
+    copies = [
+        pltpu.make_async_copy(src, dst, sems.at[k])
+        for k, (src, dst) in enumerate(zip(refs[:half], refs[half:-1]))
+    ]
+    for copy in copies:
+        copy.start()
+    for copy in copies:
+        copy.wait()
 
 
 def fused_device(
@@ -501,23 +565,30 @@
         V((steps, channels, hid), BF), V((channels, hid), F32), V((channels, hid), F32),
         V((steps, hid, channels), BF), V((hid, channels), F32), V((hid, channels), F32),
         V((steps, hid, channels), BF), V((steps, hid, channels), BF),
-        V((steps, channels, hid), BF), V((steps, channels, hid), BF),
-        V((half, hid), BF), V((half, hid), BF),
-        pltpu.SemaphoreType.DMA((40,)), pltpu.SemaphoreType.DMA((40,)),
+        V((steps, hid // CUT, channels, CUT), BF), V((steps, hid // CUT, channels, CUT), BF),
+        V((hid // CUT, half, CUT), BF), V((hid // CUT, half, CUT), BF),
+        V((channels, 2 * rows), BF), V((channels, hid), F32), V((half, 2 * hid), F32),
+        pltpu.SemaphoreType.DMA((48,)), pltpu.SemaphoreType.DMA((48,)),
+        pltpu.SemaphoreType.DMA((3,)),
     ]
     shapes = [
-        jax.ShapeDtypeStruct((taps, half), F32),
-        jax.ShapeDtypeStruct(chan_vec.shape[1:], F32),
+        jax.ShapeDtypeStruct((taps, 1, half), F32),
+        jax.ShapeDtypeStruct((chan_vec.shape[1], 1, half), F32),
         jax.ShapeDtypeStruct(w_in.shape[1:], F32),
         jax.ShapeDtypeStruct((1, hid), F32),
         jax.ShapeDtypeStruct(w_out.shape[1:], F32),
         jax.ShapeDtypeStruct((rows, channels), BF),
     ]
     whole = pl.BlockSpec(memory_space=pltpu.VMEM)
+    left = pl.BlockSpec(memory_space=pl.ANY)
+
+    def rows_apart(value):
+        return value.transpose(1, 0, 2)
+
     out = pl.pallas_call(
         lambda *refs: fused_kernel((height, width, channels, hid), *refs),
         out_shape=shapes,
-        in_specs=[whole] * 12,
+        in_specs=[whole] * 6 + [left] + [whole] * 2 + [left, whole, left],
         out_specs=[whole] * 6,
         scratch_shapes=scratch,
         compiler_params=pltpu.CompilerParams(
@@ -525,11 +596,19 @@
         ),
     )(
         images.reshape(steps, rows, channels), cotangent.reshape(steps, rows, channels),
-        dw_kernel[0], chan_vec[0], w_in[0], b_in, w_out[0],
-        mom_kernel[0], mom_chan[0], mom_in[0], mom_bin, mom_out[0],
-    )
+        rows_apart(dw_kernel), rows_apart(chan_vec), w_in[0], b_in, w_out[0],
+        rows_apart(mom_kernel), rows_apart(mom_chan), mom_in[0], mom_bin, mom_out[0],
+    )
+    out = pl.pallas_call(
+        write_results,
+        out_shape=shapes,
+        in_specs=[pl.BlockSpec(memory_space=pltpu.HBM)] * 6,
+        out_specs=[pl.BlockSpec(memory_space=pltpu.HBM)] * 6,
+        scratch_shapes=[pltpu.SemaphoreType.DMA((6,))],
+        compiler_params=pltpu.CompilerParams(vmem_limit_bytes=60 * 2**20),
+    )(*out)
     return (
-        out[0][None], out[1][None], out[2][None], out[3], out[4][None],
+        rows_apart(out[0]), rows_apart(out[1]), out[2][None], out[3], out[4][None],
         out[5].reshape(1, 1, height, width, channels),
     )
 

time: 108 us -> 163 us (1.51)
  Pallas kernels: 96.6 us -> 162 us
  local copies, waits for them, and re-layouts: 10.4 us -> 0 us
    pallas_call x0 -> x1, Pallas kernels: none -> 80.4 us  [fused_device(): pl.pallas_call(write_results, out_shape=shapes, in_specs=[pl.BlockSpec(me...]
    pallas_call x1, Pallas kernels: 96.6 us -> 81.5 us  [fused_device(): pl.pallas_call(lambda *refs: fused_kernel((height, width, channels, hid),...]
    unnamed x14 -> x0, local copies, waits for them, and re-layouts: 10.4 us -> none
where the time goes in v1:
time: 163 us
  Pallas kernels  162 us (99%)
    pallas_call x1, Pallas kernels, fused_device(): pl.pallas_call(lambda *refs: fused_kernel((height, width, channels, hid),...  81.5 us
    pallas_call x1, Pallas kernels, fused_device(): pl.pallas_call(write_results, out_shape=shapes, in_specs=[pl.BlockSpec(me...  80.4 us

profile of v1, /device:TPU:0, one launch (start us, length us, event | category | flops | bytes accessed | tf_op | source)
XLA Modules:
  0.0 162.5 jit_solution(17025556373059851942)
XLA Ops:
  0.6 81.5 %shard_map.163 = (f32[49,1,192]{2,1,0:T(1,128)}, f32[5,1,192]{2,1,0:T(1,128)}, f32[192,1536]{1,0:T(8,128)}, f32[1,768]{1,0:T(1,128)}, f32[768,384]{1,0:T(8,128)}, /*index=5*/bf16[256,384]{1,0:T(8,128)(2,1)}) custom-call(bf16[2,256,384]{2,1,0:T(8,128)(2,1)} %bitcast.19, bf16[2,256,384]{2,1,0:T(8,128)(2,1)} %bitcast.20, f32[49,1,192]{2,1,0:T(1,128)} %bitcast.21, ...), custom_call_target="tpu_custom_call" | custom-call | tf_op jit(solution)/shard_map/pallas_call | solution.py:588
  82.2 80.4 %shard_map.164 = (f32[49,1,192]{2,1,0:T(1,128)}, f32[5,1,192]{2,1,0:T(1,128)}, f32[192,1536]{1,0:T(8,128)}, f32[1,768]{1,0:T(1,128)}, f32[768,384]{1,0:T(8,128)}, /*index=5*/bf16[256,384]{1,0:T(8,128)(2,1)}) custom-call(f32[49,1,192]{2,1,0:T(1,128)} %get-tuple-element.18.refs_0_, f32[5,1,192]{2,1,0:T(1,128)} %get-tuple-element.19.refs_1_, ...), custom_call_target="tpu_custom_call" | custom-call | tf_op jit(solution)/shard_map/pallas_call | solution.py:602

commit v2 on v1

--- a/solution.py
+++ b/solution.py
@@ -239,7 +239,11 @@
     w_stage[...] = win_ref[:, their_cols].astype(BF)
     pl.semaphore_wait(barrier, 1 + STEPS)
     small_copy = push(small_mine.at[0], small_theirs.at[0], pair)
-    w_copy = push(w_stage, w_in_low.at[0, my_rows, :], pair)
+    cuts = [slice(c * CUT, (c + 1) * CUT) for c in range(hid // CUT)]
+    early = len(cuts) - 1
+    w_copies = [
+        push(w_stage.at[:, cut], w_in_low.at[0, my_rows, cut], pair) for cut in cuts[:early]
+    ]
     small_mine[1, 0:taps, :] = mkernel_ref[:, 0, :]
     small_mine[1, CHAN_ROW : CHAN_ROW + 5, :] = mchan_ref[:, 0, :]
 
@@ -289,29 +293,21 @@
             copies.append(push(normed.at[step, at], normed.at[step, theirs], pair))
         return copies
 
-    def through(step, place, after=None):
+    def begin(step, place):
         at = slice(place * rows, (place + 1) * rows)
         scale = small_p[CHAN_ROW + 4 : CHAN_ROW + 5, :]
         cot = (cot_ref[step] if place == 0 else cot_theirs[step]).astype(F32)
         dmlp[at, :] = (cot * scale).astype(BF)
-
-        def body(c, _):
-            cut = pl.ds(pl.multiple_of(c * CUT, CUT), CUT)
-            pre = dot(normed[step, at, :], w_in_low[step, :, cut]) + bias_p[0:1, cut]
-            bell = 0.5 * (1.0 + lax.erf(pre * SQRT_HALF))
-            hidden[at, cut] = (pre * bell).astype(BF)
-            slope = bell + pre * jnp.exp(-0.5 * pre * pre) * INV_ROOT_TWO_PI
-            dhid = dot(dmlp[at, :], w_out_low[step, cut, :], 1, 1)
-            dpre[at, cut] = (dhid * slope).astype(BF)
-            return 0
-
-        if after is None:
-            lax.fori_loop(0, hid // CUT, body, 0)
-        else:
-            for c in range(hid // CUT):
-                body(c, 0)
-                after(c)
         return cot, at
+
+    def chunk(step, at, c):
+        cut = slice(c * CUT, (c + 1) * CUT)
+        pre = dot(normed[step, at, :], w_in_low[step, :, cut]) + bias_p[0:1, cut]
+        bell = 0.5 * (1.0 + lax.erf(pre * SQRT_HALF))
+        hidden[at, cut] = (pre * bell).astype(BF)
+        slope = bell + pre * jnp.exp(-0.5 * pre * pre) * INV_ROOT_TWO_PI
+        dhid = dot(dmlp[at, :], w_out_low[step, cut, :], 1, 1)
+        dpre[at, cut] = (dhid * slope).astype(BF)
 
     def in_update(step, c, grad):
         cut = slice(c * CUT, (c + 1) * CUT)
@@ -360,7 +356,13 @@
             cot_copy = push(cot_ref.at[0], cot_theirs.at[0], pair)
             loads[0].wait()
             w_out_low[0] = w_out_full[...].astype(BF)
-            w_copy.wait_recv()
+            for cut in cuts[early:]:
+                w_copies.append(push(w_stage.at[:, cut], w_in_low.at[0, my_rows, cut], pair))
+            loads[2].wait()
+            m_in_full[my_rows, :] = m_in_rows[:, my_cols]
+            m_stage[...] = m_in_rows[:, their_cols].astype(BF)
+            m_copies = [push(m_stage.at[:, cut], m_theirs.at[:, cut], pair) for cut in cuts[:-1]]
+            w_copies[0].wait_recv()
         else:
             for c, copy in enumerate(gossip["out"]):
                 cut = slice(c * CUT, (c + 1) * CUT)
@@ -379,46 +381,71 @@
         onward = (lax.rem(me + 2**step, peers), grp)
         gossip = {"out": [], "in": []}
 
-        cot, at = through(step, 0)
+        other_at = slice(rows, 2 * rows)
+
+        def meet():
+            for copy in normed_copies:
+                copy.wait_recv()
+            normed_t[:, other_at] = normed[step, other_at, :].T
+            cot_copy.wait_recv()
+            return begin(step, 1)
+
+        cot, at = begin(step, 0)
+        chunk(step, at, 0)
+        if step == 0:
+            normed_t[:, at] = normed[step, at, :].T
+            other_cot, _ = meet()
+            chunk(step, other_at, 0)
+        for c in range(1, len(cuts)):
+            if step == 0:
+                w_copies[c].wait_recv()
+            chunk(step, at, c)
+            if step == 0:
+                chunk(step, other_at, c)
+        final = step == STEPS - 1
+        if step == 0:
+            dnorm_out[step] = dot(dpre[other_at, :], w_in_low[step], 1, 1).astype(BF)
+            dnorm_copy = push(dnorm_out.at[step], dnorm_in.at[step], pair)
+            m_copies.append(push(m_stage.at[:, cuts[-1]], m_theirs.at[:, cuts[-1]], pair))
+            small_m_copy = push(small_mine.at[1], small_theirs.at[1], pair)
         dnorm_mine[...] = dot(dpre[at, :], w_in_low[step], 1, 1)
         mlp = dot(hidden[at, :], w_out_low[step])
         mlp_ref[...] = mlp
-        normed_t[:, at] = normed[step, at, :].T
+        if step > 0:
+            normed_t[:, at] = normed[step, at, :].T
         scale_grad = jnp.sum(cot * mlp, axis=0, keepdims=True)
         cot_sum = jnp.sum(cot, axis=0, keepdims=True)
         scale_grad = scale_grad + cot_sum * small_p[CHAN_ROW + 3 : CHAN_ROW + 4, :]
         bias_grad = jnp.sum(cot * small_p[CHAN_ROW + 4 : CHAN_ROW + 5, :], axis=0, keepdims=True)
         if step == 0:
             loads[1].wait()
-            loads[2].wait()
-            m_in_full[my_rows, :] = m_in_rows[:, my_cols]
-            m_stage[...] = m_in_rows[:, their_cols].astype(BF)
-
-        for copy in normed_copies:
-            copy.wait_recv()
-        normed_t[:, rows : 2 * rows] = normed[step, rows : 2 * rows, :].T
-        cot_copy.wait_recv()
-        final = step == STEPS - 1
-        after = (lambda c: in_update(step, c, in_gradient(step, c))) if final else None
-        cot, at = through(step, 1, after)
-        dnorm_out[step] = dot(dpre[at, :], w_in_low[step], 1, 1).astype(BF)
-        dnorm_copy = push(dnorm_out.at[step], dnorm_in.at[step], pair)
+            w_in_full[their_rows, :] = w_in_low[0, their_rows, :].astype(F32)
+        else:
+            other_cot, _ = meet()
+            for c in range(len(cuts)):
+                chunk(step, other_at, c)
+                if final:
+                    in_update(step, c, in_gradient(step, c))
+            dnorm_out[step] = dot(dpre[other_at, :], w_in_low[step], 1, 1).astype(BF)
+            dnorm_copy = push(dnorm_out.at[step], dnorm_in.at[step], pair)
         out_updates(step)
-        mlp = dot(hidden[at, :], w_out_low[step])
-        scale_grad = scale_grad + jnp.sum(cot * mlp, axis=0, keepdims=True)
+        mlp = dot(hidden[other_at, :], w_out_low[step])
+        scale_grad = scale_grad + jnp.sum(other_cot * mlp, axis=0, keepdims=True)
         bias_update(step)
         if final:
             mlp_out[...] = mlp.astype(BF)
         else:
-            for c in range(hid // CUT):
-                in_grad[:, c * CUT : (c + 1) * CUT] = in_gradient(step, c)
+            for c, cut in enumerate(cuts):
+                if c == len(cuts) - 1:
+                    in_grad[:, cut] = in_gradient(step, c)
+                else:
+                    m_copies[c].wait_recv()
+                    m_in_full[their_rows, cut] = m_theirs[:, cut].astype(F32)
+                    in_update(step, c, in_gradient(step, c))
 
         dnorm_copy.wait_recv()
         if final:
             mlp_copy = push(mlp_out, mlp_in, pair)
-        else:
-            small_m_copy = push(small_mine.at[1], small_theirs.at[1], pair)
-            m_copy = push(m_stage, m_theirs, pair)
         gain = small_p[CHAN_ROW + 1 : CHAN_ROW + 2, :]
         zero = jnp.zeros((1, channels), F32)
 
@@ -479,11 +506,9 @@
         gossip_small_out[step] = stepped.astype(BF)
         small_gossip = push(gossip_small_out.at[step], gossip_small_in.at[step], onward)
         if step + 1 < STEPS:
-            m_copy.wait_recv()
-            m_in_full[their_rows, :] = m_theirs[...].astype(F32)
-            w_in_full[their_rows, :] = w_in_low[0, their_rows, :].astype(F32)
-            for c in range(hid // CUT):
-                in_update(step, c, in_grad[:, c * CUT : (c + 1) * CUT])
+            m_copies[-1].wait_recv()
+            m_in_full[their_rows, cuts[-1]] = m_theirs[:, cuts[-1]].astype(F32)
+            in_update(step, len(cuts) - 1, in_grad[:, cuts[-1]])
             cot_copy = push(cot_ref.at[step + 1], cot_theirs.at[step + 1], pair)
         if not final:
             small_gossip.wait_recv()
@@ -523,16 +548,18 @@
 
 
 def write_results(*refs):
-    sems = refs[-1]
-    half = (len(refs) - 1) // 2
-    copies = [
-        pltpu.make_async_copy(src, dst, sems.at[k])
-        for k, (src, dst) in enumerate(zip(refs[:half], refs[half:-1]))
-    ]
-    for copy in copies:
-        copy.start()
-    for copy in copies:
-        copy.wait()
+    count = (len(refs) - 2) // 3
+    srcs, dsts, holds = refs[:count], refs[count : 2 * count], refs[2 * count : 3 * count]
+    read_sem, write_sem = refs[-2:]
+    reads = [pltpu.make_async_copy(a, b, read_sem.at[k]) for k, (a, b) in enumerate(zip(srcs, holds))]
+    writes = [pltpu.make_async_copy(a, b, write_sem.at[k]) for k, (a, b) in enumerate(zip(holds, dsts))]
+    for read in reads:
+        read.start()
+    for read, write in zip(reads, writes):
+        read.wait()
+        write.start()
+    for write in writes:
+        write.wait()
 
 
 def fused_device(
@@ -604,7 +631,8 @@
         out_shape=shapes,
         in_specs=[pl.BlockSpec(memory_space=pltpu.HBM)] * 6,
         out_specs=[pl.BlockSpec(memory_space=pltpu.HBM)] * 6,
-        scratch_shapes=[pltpu.SemaphoreType.DMA((6,))],
+        scratch_shapes=[V(x.shape, x.dtype) for x in shapes]
+        + [pltpu.SemaphoreType.DMA((6,)), pltpu.SemaphoreType.DMA((6,))],
         compiler_params=pltpu.CompilerParams(vmem_limit_bytes=60 * 2**20),
     )(*out)
     return (

time: 163 us -> 86 us (0.53)
  Pallas kernels: 162 us -> 85.2 us
    pallas_call x1, Pallas kernels: 80.4 us -> 2.88 us  [fused_device(): pl.pallas_call(write_results, out_shape=shapes, in_specs=[pl.BlockSpec(me...]
where the time goes in v2:
time: 86 us; the launch traced here: 85.8 us
  Pallas kernels  85.2 us (99%)
    pallas_call x1, Pallas kernels, fused_device(): pl.pallas_call(lambda *refs: fused_kernel((height, width, channels, hid),...  82.3 us
    pallas_call x1, Pallas kernels, fused_device(): pl.pallas_call(write_results, out_shape=shapes, in_specs=[pl.BlockSpec(me...  2.88 us

profile of v2, /device:TPU:0, one launch (start us, length us, event | category | flops | bytes accessed | tf_op | source)
XLA Modules:
  0.0 85.8 jit_solution(8544031686542412250)
XLA Ops:
  0.6 82.3 %shard_map.163 = (f32[49,1,192]{2,1,0:T(1,128)}, f32[5,1,192]{2,1,0:T(1,128)}, f32[192,1536]{1,0:T(8,128)}, f32[1,768]{1,0:T(1,128)}, f32[768,384]{1,0:T(8,128)}, /*index=5*/bf16[256,384]{1,0:T(8,128)(2,1)}) custom-call(bf16[2,256,384]{2,1,0:T(8,128)(2,1)} %bitcast.19, bf16[2,256,384]{2,1,0:T(8,128)(2,1)} %bitcast.20, f32[49,1,192]{2,1,0:T(1,128)} %bitcast.21, ...), custom_call_target="tpu_custom_call" | custom-call | tf_op jit(solution)/shard_map/pallas_call | solution.py:615
  82.9 2.9 %shard_map.164 = (f32[49,1,192]{2,1,0:T(1,128)}, f32[5,1,192]{2,1,0:T(1,128)}, f32[192,1536]{1,0:T(8,128)}, f32[1,768]{1,0:T(1,128)}, f32[768,384]{1,0:T(8,128)}, /*index=5*/bf16[256,384]{1,0:T(8,128)(2,1)}) custom-call(f32[49,1,192]{2,1,0:T(1,128)} %get-tuple-element.18.refs_0_, f32[5,1,192]{2,1,0:T(1,128)} %get-tuple-element.19.refs_1_, ...), custom_call_target="tpu_custom_call" | custom-call | tf_op jit(solution)/shard_map/pallas_call | solution.py:629

commit v3 on v2

--- a/solution.py
+++ b/solution.py
@@ -286,9 +286,9 @@
             return 0
 
         copies = []
-        for h in range(2):
-            lax.fori_loop(h * height // 2, (h + 1) * height // 2, body, 0)
-            at = slice(h * rows // 2, (h + 1) * rows // 2)
+        for h in range(4):
+            lax.fori_loop(h * height // 4, (h + 1) * height // 4, body, 0)
+            at = slice(h * rows // 4, (h + 1) * rows // 4)
             theirs = slice(rows + at.start, rows + at.stop)
             copies.append(push(normed.at[step, at], normed.at[step, theirs], pair))
         return copies

time: 86 us -> 84.3 us (0.980)
  Pallas kernels: 85.2 us -> 83.5 us
    pallas_call x1, Pallas kernels: 82.3 us -> 80.6 us  [fused_device(): pl.pallas_call(lambda *refs: fused_kernel((height, width, channels, hid),...]
where the time goes in v3:
time: 84.3 us; the launch traced here: 84.2 us
  Pallas kernels  83.5 us (99%)
    pallas_call x1, Pallas kernels, fused_device(): pl.pallas_call(lambda *refs: fused_kernel((height, width, channels, hid),...  80.6 us
    pallas_call x1, Pallas kernels, fused_device(): pl.pallas_call(write_results, out_shape=shapes, in_specs=[pl.BlockSpec(me...  2.88 us

profile of v3, /device:TPU:0, one launch (start us, length us, event | category | flops | bytes accessed | tf_op | source)
XLA Modules:
  0.0 84.2 jit_solution(16299897210499410830)
XLA Ops:
  0.6 80.6 %shard_map.163 = (f32[49,1,192]{2,1,0:T(1,128)}, f32[5,1,192]{2,1,0:T(1,128)}, f32[192,1536]{1,0:T(8,128)}, f32[1,768]{1,0:T(1,128)}, f32[768,384]{1,0:T(8,128)}, /*index=5*/bf16[256,384]{1,0:T(8,128)(2,1)}) custom-call(bf16[2,256,384]{2,1,0:T(8,128)(2,1)} %bitcast.19, bf16[2,256,384]{2,1,0:T(8,128)(2,1)} %bitcast.20, f32[49,1,192]{2,1,0:T(1,128)} %bitcast.21, ...), custom_call_target="tpu_custom_call" | custom-call | tf_op jit(solution)/shard_map/pallas_call | solution.py:615
  81.3 2.9 %shard_map.164 = (f32[49,1,192]{2,1,0:T(1,128)}, f32[5,1,192]{2,1,0:T(1,128)}, f32[192,1536]{1,0:T(8,128)}, f32[1,768]{1,0:T(1,128)}, f32[768,384]{1,0:T(8,128)}, /*index=5*/bf16[256,384]{1,0:T(8,128)(2,1)}) custom-call(f32[49,1,192]{2,1,0:T(1,128)} %get-tuple-element.18.refs_0_, f32[5,1,192]{2,1,0:T(1,128)} %get-tuple-element.19.refs_1_, ...), custom_call_target="tpu_custom_call" | custom-call | tf_op jit(solution)/shard_map/pallas_call | solution.py:629
